TPU v7x, 32 devices: a whole 2x2x4 slice. The times are simulated.
32 devices in a mesh: groups: 2 (over y), sub: 4 (over z), rhs: 2 (over x), face: 2 (over core).
Axes of the slice: x: 2, y: 2, z: 4, core: 2. Of those that a mesh axis runs over, the one named last changes fastest.
Arguments:
- mortar_in: bfloat16 [1024, 64, 256], P(('groups', 'sub'), 'rhs'), parts along dimension 0, may hold values from -6 to 6
- pump_rate: float32 [128], P(('groups', 'rhs')), parts along dimension 0, may hold values from 4 to 16
- well_cell: int32 [128], P(('groups', 'rhs')), parts along dimension 0, may hold values from 0 to 131071
- face_owner: int32 [2048, 1], P(('groups', 'sub', 'face')), parts along dimension 0, may hold values from 0 to 3; in each aligned block of 128 rows (0 to 127, 128 to 255, ...) at most 64 rows name the same one
- face_slot: int32 [2048], P(('groups', 'sub', 'face')), parts along dimension 0, may hold values from 0 to 127
- face_scale: bfloat16 [2048, 256], P(('groups', 'sub', 'face')), parts along dimension 0, may hold values from 0.5 to 2
- section: int32 [8], P(('groups', 'sub')), parts along dimension 0, may hold values 0 or 1
- basis: bfloat16 [8, 256, 256], P(('groups', 'sub')), parts along dimension 0, may hold values from -0.375 to 0.375
- projection: bfloat16 [256, 256], replicated, may hold values from -0.375 to 0.375
Outputs:
- result: float32 [1024, 64, 256], P(('groups', 'sub', 'face'), 'rhs'), parts along dimension 0
There are 2 independent parts, one for each index of `groups`. A program takes and returns all parts, laid end to end along the dimension named above; an argument that names none is the same for every part. Nothing has to cross between parts.
Inputs may be any that keep to these rules, and one draw needn't show every extreme that they name: `face_owner`: among the 128 faces of one device no subdomain is named by more than 64 faces, a bound that some block reaches.
All inputs are finite; a program needn't handle non-finite values. No bound on the sum of `section` on one device may be relied on, other than what follows from the above.
Results may differ from a plain program's by a relative error of at most 0.004.
Values may be sent and summed in bfloat16 or wider, within the bound.
No kernel may reach another device: no remote copies, remote signals or barrier semaphores. Data moves between devices by JAX's collectives and lax.ppermute only.
A program may use at most 64 MiB of HBM per device.

v0:
```python
import functools

import jax
import jax.numpy as jnp
from jax import lax
from jax.experimental import pallas as pl
from jax.experimental.pallas import tpu as pltpu
from jax.sharding import PartitionSpec as P

ROW_TILE = 16
VMEM = pl.BlockSpec(memory_space=pltpu.VMEM)
HBM = pl.BlockSpec(memory_space=pltpu.HBM)
SMEM = pl.BlockSpec(memory_space=pltpu.SMEM)
MIB = 1024 * 1024
TILES = 4


def pack_kernel(owner_ref, slot_ref, scale_ref, section_ref, *packs):
    subdomains = len(packs)
    rows, dof_count = packs[0].shape
    rows -= ROW_TILE
    faces = owner_ref.shape[1]
    sign = (1 - 2 * section_ref[...]).astype(jnp.float32)
    shifts = lax.broadcasted_iota(jnp.int32, (subdomains, faces), 0)
    named = lax.rem(lax.axis_index("sub") + shifts, subdomains) == owner_ref[...]
    earlier = lax.broadcasted_iota(jnp.int32, (faces, faces), 0) < lax.broadcasted_iota(
        jnp.int32, (faces, faces), 1
    )
    rank = jnp.dot(
        named.astype(jnp.bfloat16), earlier.astype(jnp.bfloat16), preferred_element_type=jnp.float32
    )
    place = jnp.where(named, rank.astype(jnp.int32), -1)
    slots = slot_ref[...].astype(jnp.bfloat16)
    for shift, pack_ref in enumerate(packs):
        hit = place[shift : shift + 1, :] == lax.broadcasted_iota(jnp.int32, (rows, faces), 0)
        hit = hit.astype(jnp.bfloat16)
        packed = jnp.dot(hit, scale_ref[...], preferred_element_type=jnp.float32) * sign
        listed = lax.dot_general(
            slots, hit, (((1,), (1,)), ((), ())), preferred_element_type=jnp.float32
        )
        meta = jnp.concatenate([listed, jnp.zeros((1, dof_count - rows), jnp.float32)], axis=1)
        meta = jnp.broadcast_to(meta, (ROW_TILE, dof_count))
        pack_ref[:rows, :] = packed.astype(jnp.bfloat16)
        pack_ref[rows:, :] = meta.astype(jnp.bfloat16)


def block_weights(packs, blocks_own):
    rows = packs[0].shape[0] - ROW_TILE
    first = lax.axis_index("face") * blocks_own
    block_ids = first + lax.broadcasted_iota(jnp.int32, (blocks_own, rows), 0)
    total = None
    for pack in packs:
        slots = pack[rows:, :].astype(jnp.int32)[:1, :rows]
        hit = (slots == block_ids).astype(jnp.bfloat16)
        part = jnp.dot(hit, pack[:rows, :], preferred_element_type=jnp.float32)
        total = part if total is None else total + part
    return total


def own_kernel(mortar_ref, rate_ref, cell_ref, basis_ref, pack_ref, swapped_ref, pumped_ref, sum_ref, weight_ref, sem):
    blocks_own, columns, dof_count = pumped_ref.shape
    first_block = lax.axis_index("face") * blocks_own
    fetch = pltpu.make_async_copy(mortar_ref.at[pl.ds(first_block, blocks_own)], pumped_ref, sem)
    fetch.start()
    weight_ref[...] = block_weights((pack_ref, swapped_ref), blocks_own)
    fetch.wait()

    base = lax.axis_index("sub") * mortar_ref.shape[0] + first_block
    for column in range(columns):
        block = lax.div(cell_ref[column], dof_count) - base
        dof = lax.rem(cell_ref[column], dof_count)

        @pl.when((block >= 0) & (block < blocks_own))
        def _():
            slab = slice(column // ROW_TILE * ROW_TILE, (column // ROW_TILE + 1) * ROW_TILE)
            shape = (ROW_TILE, dof_count)
            at_well = (lax.broadcasted_iota(jnp.int32, shape, 0) == column % ROW_TILE) & (
                lax.broadcasted_iota(jnp.int32, shape, 1) == dof
            )
            well = jnp.where(at_well, rate_ref[column], 0.0)
            pumped_ref[block, slab, :] = (pumped_ref[block, slab, :].astype(jnp.float32) + well).astype(
                jnp.bfloat16
            )

    tile_blocks = blocks_own // TILES
    for tile in range(TILES):
        at = slice(tile * tile_blocks, (tile + 1) * tile_blocks)
        scaled = (pumped_ref[at].astype(jnp.float32) * weight_ref[at][:, None, :]).astype(jnp.bfloat16)
        flux = jnp.dot(
            scaled.reshape(tile_blocks * columns, dof_count), basis_ref[0], preferred_element_type=jnp.float32
        )
        sum_ref[at] = flux.reshape(tile_blocks, columns, dof_count)


def apply_kernel(groups, *refs):
    pumped_ref, sum_ref, projection_ref = refs[:3]
    bases, refs = refs[3 : 3 + 4 * len(groups)], refs[3 + 4 * len(groups) :]
    packs, (result_ref, weight_ref, basis_ref, scaled_ref, out_ref, sems) = refs[:-6], refs[-6:]
    blocks_own, columns, dof_count = pumped_ref.shape
    others = weight_ref.shape[0]
    lane = 2 * lax.rem(lax.axis_index("rhs"), 2) + lax.axis_index("face")

    def put(array, *by_lane):
        shift = jnp.int32(by_lane[3])
        for which in range(3):
            shift = jnp.where(lane == which, by_lane[which], shift)
        at = pl.multiple_of((shift - 1) * dof_count, dof_count)
        basis_ref[pl.ds(at, dof_count), :] = array[0]

    spare = others + 1
    for at, (a, b, c) in enumerate(groups):
        first, first_swapped, second, second_swapped = bases[4 * at : 4 * at + 4]
        put(first, a, spare, b, c)
        put(second, b, c, a, spare)
        put(first_swapped, spare, a, c, b)
        put(second_swapped, c, b, spare, a)
    for other in range(others):
        weight_ref[other] = block_weights(packs[2 * other : 2 * other + 2], blocks_own)

    tile_blocks = blocks_own // TILES
    copies = []
    for tile in range(TILES):
        at = slice(tile * tile_blocks, (tile + 1) * tile_blocks)
        values = pumped_ref[at].astype(jnp.float32)
        for other in range(others):
            scaled = (values * weight_ref[other, at][:, None, :]).astype(jnp.bfloat16)
            scaled_ref[tile % 2, :, other * dof_count : (other + 1) * dof_count] = scaled.reshape(
                tile_blocks * columns, dof_count
            )
        total = jnp.dot(
            scaled_ref[tile % 2], basis_ref[: others * dof_count, :], preferred_element_type=jnp.float32
        )
        total = total + sum_ref[at].reshape(tile_blocks * columns, dof_count)
        result = jnp.dot(
            total.astype(jnp.bfloat16), projection_ref[...], preferred_element_type=jnp.float32
        )
        out_ref[at] = result.reshape(tile_blocks, columns, dof_count)
        copies.append(pltpu.make_async_copy(out_ref.at[at], result_ref.at[at], sems.at[tile]))
        copies[-1].start()
    for copy in copies:
        copy.wait()


def on_device(
    mortar_in, pump_rate, well_cell, face_owner, face_slot, face_scale, section, basis, projection
):
    blocks_dev, cols_dev, dof_count = mortar_in.shape
    faces_dev = face_slot.shape[0]
    subdomains, rights, halves = lax.axis_size("sub"), lax.axis_size("rhs"), lax.axis_size("face")
    others = subdomains - 1
    blocks_own = blocks_dev // halves
    capacity = max(2, 2 * faces_dev // subdomains)
    pack_rows = -(-capacity // ROW_TILE) * ROW_TILE + ROW_TILE
    block_shape = (blocks_own, cols_dev, dof_count)

    def flat(sub, right, face):
        return ((sub % subdomains) * rights + right) * halves + face

    cells = [(s, r) for s in range(subdomains) for r in range(rights)]
    cross = [(i, i ^ 1) for i in range(rights)]
    swap = [(i, i ^ 1) for i in range(halves)]
    shifts = list(range(1, subdomains))
    if len(shifts) > 1:
        shifts[0], shifts[1] = shifts[1], shifts[0]
    groups = [tuple(shifts[i : i + 3]) for i in range(0, len(shifts), 3)]
    groups = [g + (subdomains,) * (3 - len(g)) for g in groups]
    firsts = []
    for a, b, c in groups:
        pairs = []
        for s, r in cells:
            for face, shift in ((0, b), (1, c)) if r % 2 else ((0, a),):
                if shift < subdomains:
                    pairs.append((flat(s, r, face), flat(s + shift, r, face)))
        firsts.append(lax.ppermute(basis, ("sub", "rhs", "face"), pairs))

    packs = pl.pallas_call(
        pack_kernel,
        out_shape=[jax.ShapeDtypeStruct((pack_rows, dof_count), jnp.bfloat16)] * subdomains,
        in_specs=[VMEM] * 4,
        out_specs=[VMEM] * subdomains,
        cost_estimate=pl.CostEstimate(flops=4_000_000_000, bytes_accessed=8 * MIB, transcendentals=0),
        name="pack_weights",
    )(
        face_owner.reshape(1, faces_dev),
        face_slot.reshape(1, faces_dev),
        face_scale,
        section.reshape(1, 1),
    )
    arrived = []
    for shift in range(1, subdomains):
        ring = [(i, (i + shift) % subdomains) for i in range(subdomains)]
        arrived.append(lax.ppermute(packs[shift], "sub", ring))
    own_swapped = lax.ppermute(packs[0], "face", swap)

    firsts, own_pack = lax.optimization_barrier((firsts, packs[0]))
    pumped, own_sum = pl.pallas_call(
        own_kernel,
        out_shape=[
            jax.ShapeDtypeStruct(block_shape, jnp.bfloat16),
            jax.ShapeDtypeStruct(block_shape, jnp.float32),
        ],
        in_specs=[HBM, SMEM, SMEM, VMEM, VMEM, VMEM],
        out_specs=[VMEM, VMEM],
        scratch_shapes=[pltpu.VMEM((blocks_own, dof_count), jnp.float32), pltpu.SemaphoreType.DMA(())],
        compiler_params=pltpu.CompilerParams(vmem_limit_bytes=32 * MIB),
        cost_estimate=pl.CostEstimate(flops=2_000_000_000, bytes_accessed=8 * MIB, transcendentals=0),
        name="own_blocks",
    )(mortar_in, pump_rate, well_cell, basis, own_pack, own_swapped)

    arrived, pumped = lax.optimization_barrier((arrived, pumped))
    weights = []
    for array in arrived:
        weights += [array, lax.ppermute(array, "face", swap)]

    bases = []
    for first in firsts:
        second = lax.ppermute(first, "rhs", cross)
        bases += [first, lax.ppermute(first, "face", swap), second, lax.ppermute(second, "face", swap)]

    operands = [pumped, own_sum, projection, *bases, *weights]
    return pl.pallas_call(
        functools.partial(apply_kernel, groups),
        out_shape=jax.ShapeDtypeStruct(block_shape, jnp.float32),
        in_specs=[VMEM] * len(operands),
        out_specs=HBM,
        scratch_shapes=[
            pltpu.VMEM((others, blocks_own, dof_count), jnp.float32),
            pltpu.VMEM(((others + 1) * dof_count, dof_count), jnp.bfloat16),
            pltpu.VMEM((2, blocks_own // TILES * cols_dev, others * dof_count), jnp.bfloat16),
            pltpu.VMEM(block_shape, jnp.float32),
            pltpu.SemaphoreType.DMA((TILES,)),
        ],
        compiler_params=pltpu.CompilerParams(vmem_limit_bytes=48 * MIB),
        name="apply_blocks",
    )(*operands)


def solution(mesh):
    in_specs = (
        P(("groups", "sub"), "rhs", None),
        P(("groups", "rhs")),
        P(("groups", "rhs")),
        P(("groups", "sub", "face"), None),
        P(("groups", "sub", "face")),
        P(("groups", "sub", "face"), None),
        P(("groups", "sub")),
        P(("groups", "sub"), None, None),
        P(),
    )
    out_specs = P(("groups", "sub", "face"), "rhs", None)
    return jax.shard_map(
        on_device, mesh=mesh, in_specs=in_specs, out_specs=out_specs, check_vma=False
    )
```

profile of v0, /device:TPU:0, one launch (start us, length us, event | category | flops | bytes accessed | tf_op | source)
XLA Modules:
  0.0 24.9 jit_solution(17918194453468216213)
XLA Ops:
  0.0 5.9 %collective-permute-start.3 = (bf16[1,256,256]{2,1,0:T(8,128)(2,1)}, bf16[1,256,256]{2,1,0:T(8,128)(2,1)S(1)}, u32[]{:S(2)}, u32[]{:S(2)}) collective-permute-start(bf16[1,256,256]{2,1,0:T(8,128)(2,1)} %basis_ref.1), channel_id=1, source_target_pairs={{0,8},{2,6},{3,15},{4,12},{6,10},{7,3},{8,0},{10,14},{11,7},{12,4}... | collective-permute-start | bytes 393224 | tf_op jit(solution)/shard_map/ppermute | solution.py:174
  6.6 0.0 copy-start.1
  6.6 0.0 copy-start.2
  6.6 0.0 copy-start.4
  6.6 0.0 copy-start.5
  6.6 2.0 %pack_weights.1 = (bf16[80,256]{1,0:T(8,128)(2,1)}, bf16[80,256]{1,0:T(8,128)(2,1)}, bf16[80,256]{1,0:T(8,128)(2,1)}, bf16[80,256]{1,0:T(8,128)(2,1)}) custom-call(s32[1,128]{1,0:T(1,128)} %bitcast.4, s32[1,128]{1,0:T(1,128)} %bitcast.5, bf16[128,256]{1,0:T(8,128)(2,1)} %scale_ref.1, s32[1,1]{1,0:T(1,128)} %bitcast.3.section_ref), custom_call_target="tpu_custom_call" | custom-call | flops 4000000000 | bytes 8388608 | tf_op jit(solution)/shard_map/pack_weights/pallas_call | solution.py:176
  8.6 0.5 %collective-permute-done.3.refs_3_ = bf16[1,256,256]{2,1,0:T(8,128)(2,1)S(1)} collective-permute-done((bf16[1,256,256]{2,1,0:T(8,128)(2,1)}, bf16[1,256,256]{2,1,0:T(8,128)(2,1)S(1)}, u32[]{:S(2)}, u32[]{:S(2)}) %collective-permute-start.3) | collective-permute-done | bytes 131104 | tf_op jit(solution)/shard_map/ppermute | solution.py:174
  9.1 3.2 %collective-permute-start.6 = (bf16[1,256,256]{2,1,0:T(8,128)(2,1)S(1)}, bf16[1,256,256]{2,1,0:T(8,128)(2,1)S(1)}, u32[]{:S(2)}, u32[]{:S(2)}) collective-permute-start(bf16[1,256,256]{2,1,0:T(8,128)(2,1)S(1)} %collective-permute-done.3.refs_3_), channel_id=1, source_target_pairs={{0,2},{2,0},{1,3},{3,1},{4,6},{6,4},{5,7},{7,5},{8,10},{10,8},{9,1... | collective-permute-start | bytes 393224 | tf_op jit(solution)/shard_map/ppermute | solution.py:217
  12.3 0.0 collective-permute-start.4
  12.3 0.0 collective-permute-start
  12.3 3.3 %collective-permute-start.1 = (bf16[80,256]{1,0:T(8,128)(2,1)}, bf16[80,256]{1,0:T(8,128)(2,1)S(1)}, u32[]{:S(2)}, u32[]{:S(2)}) collective-permute-start(bf16[80,256]{1,0:T(8,128)(2,1)} %get-tuple-element.18), channel_id=1, source_target_pairs={{0,8},{4,12},{8,0},{12,4},{1,9},{5,13},{9,1},{13,5},{2,10},{6,14},... | collective-permute-start | bytes 122888 | tf_op jit(solution)/shard_map/ppermute | solution.py:192
  15.6 0.0 copy-start
  15.6 1.3 %collective-permute-start.2 = (bf16[80,256]{1,0:T(8,128)(2,1)}, bf16[80,256]{1,0:T(8,128)(2,1)S(1)}, u32[]{:S(2)}, u32[]{:S(2)}) collective-permute-start(bf16[80,256]{1,0:T(8,128)(2,1)} %get-tuple-element.19), channel_id=1, source_target_pairs={{0,12},{4,0},{8,4},{12,8},{1,13},{5,1},{9,5},{13,9},{2,14},{6,2},{... | collective-permute-start | bytes 122888 | tf_op jit(solution)/shard_map/ppermute | solution.py:192
  16.9 0.0 collective-permute-done.4.swapped_ref
  16.9 0.0 collective-permute-start.5
  16.9 0.0 collective-permute-done.6.refs_5_
  16.9 0.5 %collective-permute-start.7 = (bf16[1,256,256]{2,1,0:T(8,128)(2,1)S(1)}, bf16[1,256,256]{2,1,0:T(8,128)(2,1)S(1)}, u32[]{:S(2)}, u32[]{:S(2)}) collective-permute-start(bf16[1,256,256]{2,1,0:T(8,128)(2,1)S(1)} %collective-permute-done.6.refs_5_), channel_id=1, source_target_pairs={{0,1},{1,0},{2,3},{3,2},{4,5},{5,4},{6,7},{7,6},{8,9},{9,8},{10,11... | collective-permute-start | bytes 393224 | tf_op jit(solution)/shard_map/ppermute | solution.py:218
  17.4 0.0 copy-done.1
  17.4 0.0 copy-done.2
  17.4 0.0 copy-done.4
  17.5 0.0 copy-done.5
  17.5 0.0 copy-start.3
  17.5 0.8 %copy-done.3 = bf16[80,256]{1,0:T(8,128)(2,1)S(1)} copy-done((bf16[80,256]{1,0:T(8,128)(2,1)S(1)}, bf16[80,256]{1,0:T(8,128)(2,1)}, u32[]{:S(2)}) %copy-start.3) | copy-done | bytes 40984
  18.2 1.6 %own_blocks.1 = (bf16[64,32,256]{2,1,0:T(8,128)(2,1)S(1)}, f32[64,32,256]{2,1,0:T(8,128)S(1)}) custom-call(bf16[128,32,256]{2,1,0:T(8,128)(2,1)S(1)} %copy-done.1, f32[32]{0:T(128)S(1)} %copy-done.4, s32[32]{0:T(128)S(1)} %copy-done.5, bf16[1,256,256]{2,1,0:T(8,128)(2,1)S(1)} %copy-done.2, bf16[80,256]{1,0:T(8,128)(2,1)S(1)} %copy-done.3, ...), custom_call_target="tpu_custom_call" | custom-call | flops 2000000000 | bytes 8388608 | tf_op jit(solution)/shard_map/own_blocks/pallas_call | solution.py:196
  19.9 0.0 collective-permute-done.refs_7_
  19.9 0.0 collective-permute-done.1.refs_9_
  19.9 0.1 collective-permute-done.2.refs_11_
  19.9 0.1 collective-permute-start.8
  20.0 0.4 %collective-permute-start.9 = (bf16[80,256]{1,0:T(8,128)(2,1)S(1)}, bf16[80,256]{1,0:T(8,128)(2,1)S(1)}, u32[]{:S(2)}, u32[]{:S(2)}) collective-permute-start(bf16[80,256]{1,0:T(8,128)(2,1)S(1)} %collective-permute-done.1.refs_9_), channel_id=1, source_target_pairs={{0,1},{1,0},{2,3},{3,2},{4,5},{5,4},{6,7},{7,6},{8,9},{9,8},{10,11... | collective-permute-start | bytes 122888 | tf_op jit(solution)/shard_map/ppermute | solution.py:213
  20.5 0.1 collective-permute-start.10
  20.5 0.6 %collective-permute-done.8.refs_8_ = bf16[80,256]{1,0:T(8,128)(2,1)S(1)} collective-permute-done((bf16[80,256]{1,0:T(8,128)(2,1)S(1)}, bf16[80,256]{1,0:T(8,128)(2,1)S(1)}, u32[]{:S(2)}, u32[]{:S(2)}) %collective-permute-start.8) | collective-permute-done | bytes 40992 | tf_op jit(solution)/shard_map/ppermute | solution.py:213
  21.2 0.2 collective-permute-done.9.refs_10_
  21.3 0.3 %collective-permute-done.10.refs_12_ = bf16[80,256]{1,0:T(8,128)(2,1)S(1)} collective-permute-done((bf16[80,256]{1,0:T(8,128)(2,1)S(1)}, bf16[80,256]{1,0:T(8,128)(2,1)S(1)}, u32[]{:S(2)}, u32[]{:S(2)}) %collective-permute-start.10) | collective-permute-done | bytes 40992 | tf_op jit(solution)/shard_map/ppermute | solution.py:213
  21.7 0.0 collective-permute-done.5.refs_4_
  21.7 0.0 collective-permute-done.7.refs_6_
  21.7 0.0 copy-done
  21.7 3.2 %apply_blocks.1 = f32[64,32,256]{2,1,0:T(8,128)} custom-call(bf16[64,32,256]{2,1,0:T(8,128)(2,1)S(1)} %get-tuple-element.23.refs_0_, f32[64,32,256]{2,1,0:T(8,128)S(1)} %get-tuple-element.24.refs_1_, bf16[256,256]{1,0:T(8,128)(2,1)S(1)} %copy-done, bf16[1,256,256]{2,1,0:T(8,128)(2,1)S(1)} %collective-permute-done.3.refs_3_, ...), custom_call_target="tpu_custom_call" | custom-call | tf_op jit(solution)/shard_map/apply_blocks/pallas_call | solution.py:221
Async XLA Ops:
  0.0 9.1 %collective-permute-start.3 = (bf16[1,256,256]{2,1,0:T(8,128)(2,1)}, bf16[1,256,256]{2,1,0:T(8,128)(2,1)S(1)}, u32[]{:S(2)}, u32[]{:S(2)}) collective-permute-start(bf16[1,256,256]{2,1,0:T(8,128)(2,1)} %basis_ref.1), channel_id=1, source_target_pairs={{0,8},{2,6},{3,15},{4,12},{6,10},{7,3},{8,0},{10,14},{11,7},{12,4}... | collective-permute-start | bytes 393224 | tf_op jit(solution)/shard_map/ppermute | solution.py:174
  6.6 10.9 %copy-start.1 = (bf16[128,32,256]{2,1,0:T(8,128)(2,1)S(1)}, bf16[128,32,256]{2,1,0:T(8,128)(2,1)}, u32[]{:S(2)}) copy-start(bf16[128,32,256]{2,1,0:T(8,128)(2,1)} %mortar_ref.1) | copy-start | bytes 6291460
  6.6 10.9 %copy-start.2 = (bf16[1,256,256]{2,1,0:T(8,128)(2,1)S(1)}, bf16[1,256,256]{2,1,0:T(8,128)(2,1)}, u32[]{:S(2)}) copy-start(bf16[1,256,256]{2,1,0:T(8,128)(2,1)} %basis_ref.1) | copy-start | bytes 393220
  6.6 10.8 %copy-start.4 = (f32[32]{0:T(128)S(1)}, f32[32]{0:T(128)}, u32[]{:S(2)}) copy-start(f32[32]{0:T(128)} %rate_ref.1) | copy-start | bytes 388
  6.6 10.8 %copy-start.5 = (s32[32]{0:T(128)S(1)}, s32[32]{0:T(128)}, u32[]{:S(2)}) copy-start(s32[32]{0:T(128)} %cell_ref.1) | copy-start | bytes 388
  9.1 7.8 %collective-permute-start.6 = (bf16[1,256,256]{2,1,0:T(8,128)(2,1)S(1)}, bf16[1,256,256]{2,1,0:T(8,128)(2,1)S(1)}, u32[]{:S(2)}, u32[]{:S(2)}) collective-permute-start(bf16[1,256,256]{2,1,0:T(8,128)(2,1)S(1)} %collective-permute-done.3.refs_3_), channel_id=1, source_target_pairs={{0,2},{2,0},{1,3},{3,1},{4,6},{6,4},{5,7},{7,5},{8,10},{10,8},{9,1... | collective-permute-start | bytes 393224 | tf_op jit(solution)/shard_map/ppermute | solution.py:217
  12.3 4.6 %collective-permute-start.4 = (bf16[80,256]{1,0:T(8,128)(2,1)}, bf16[80,256]{1,0:T(8,128)(2,1)S(1)}, u32[]{:S(2)}, u32[]{:S(2)}) collective-permute-start(bf16[80,256]{1,0:T(8,128)(2,1)} %get-tuple-element.21.pack_ref), channel_id=1, source_target_pairs={{0,1},{1,0},{2,3},{3,2},{4,5},{5,4},{6,7},{7,6},{8,9},{9,8},{10,11... | collective-permute-start | bytes 122888 | tf_op jit(solution)/shard_map/ppermute | solution.py:193
  12.3 7.6 %collective-permute-start = (bf16[80,256]{1,0:T(8,128)(2,1)}, bf16[80,256]{1,0:T(8,128)(2,1)S(1)}, u32[]{:S(2)}, u32[]{:S(2)}) collective-permute-start(bf16[80,256]{1,0:T(8,128)(2,1)} %get-tuple-element.17), channel_id=1, source_target_pairs={{0,4},{4,8},{8,12},{12,0},{1,5},{5,9},{9,13},{13,1},{2,6},{6,10},{... | collective-permute-start | bytes 122888 | tf_op jit(solution)/shard_map/ppermute | solution.py:192
  12.3 7.6 %collective-permute-start.1 = (bf16[80,256]{1,0:T(8,128)(2,1)}, bf16[80,256]{1,0:T(8,128)(2,1)S(1)}, u32[]{:S(2)}, u32[]{:S(2)}) collective-permute-start(bf16[80,256]{1,0:T(8,128)(2,1)} %get-tuple-element.18), channel_id=1, source_target_pairs={{0,8},{4,12},{8,0},{12,4},{1,9},{5,13},{9,1},{13,5},{2,10},{6,14},... | collective-permute-start | bytes 122888 | tf_op jit(solution)/shard_map/ppermute | solution.py:192
  15.6 6.1 %copy-start = (bf16[256,256]{1,0:T(8,128)(2,1)S(1)}, bf16[256,256]{1,0:T(8,128)(2,1)}, u32[]{:S(2)}) copy-start(bf16[256,256]{1,0:T(8,128)(2,1)} %refs_2_.1) | copy-start | bytes 393220
  15.6 4.4 %collective-permute-start.2 = (bf16[80,256]{1,0:T(8,128)(2,1)}, bf16[80,256]{1,0:T(8,128)(2,1)S(1)}, u32[]{:S(2)}, u32[]{:S(2)}) collective-permute-start(bf16[80,256]{1,0:T(8,128)(2,1)} %get-tuple-element.19), channel_id=1, source_target_pairs={{0,12},{4,0},{8,4},{12,8},{1,13},{5,1},{9,5},{13,9},{2,14},{6,2},{... | collective-permute-start | bytes 122888 | tf_op jit(solution)/shard_map/ppermute | solution.py:192
  16.9 4.8 %collective-permute-start.5 = (bf16[1,256,256]{2,1,0:T(8,128)(2,1)S(1)}, bf16[1,256,256]{2,1,0:T(8,128)(2,1)S(1)}, u32[]{:S(2)}, u32[]{:S(2)}) collective-permute-start(bf16[1,256,256]{2,1,0:T(8,128)(2,1)S(1)} %collective-permute-done.3.refs_3_), channel_id=1, source_target_pairs={{0,1},{1,0},{2,3},{3,2},{4,5},{5,4},{6,7},{7,6},{8,9},{9,8},{10,11... | collective-permute-start | bytes 393224 | tf_op jit(solution)/shard_map/ppermute | solution.py:218
  16.9 4.8 %collective-permute-start.7 = (bf16[1,256,256]{2,1,0:T(8,128)(2,1)S(1)}, bf16[1,256,256]{2,1,0:T(8,128)(2,1)S(1)}, u32[]{:S(2)}, u32[]{:S(2)}) collective-permute-start(bf16[1,256,256]{2,1,0:T(8,128)(2,1)S(1)} %collective-permute-done.6.refs_5_), channel_id=1, source_target_pairs={{0,1},{1,0},{2,3},{3,2},{4,5},{5,4},{6,7},{7,6},{8,9},{9,8},{10,11... | collective-permute-start | bytes 393224 | tf_op jit(solution)/shard_map/ppermute | solution.py:218
  17.5 0.8 %copy-start.3 = (bf16[80,256]{1,0:T(8,128)(2,1)S(1)}, bf16[80,256]{1,0:T(8,128)(2,1)}, u32[]{:S(2)}) copy-start(bf16[80,256]{1,0:T(8,128)(2,1)} %get-tuple-element.21.pack_ref) | copy-start | bytes 122884
  19.9 1.2 %collective-permute-start.8 = (bf16[80,256]{1,0:T(8,128)(2,1)S(1)}, bf16[80,256]{1,0:T(8,128)(2,1)S(1)}, u32[]{:S(2)}, u32[]{:S(2)}) collective-permute-start(bf16[80,256]{1,0:T(8,128)(2,1)S(1)} %collective-permute-done.refs_7_), channel_id=1, source_target_pairs={{0,1},{1,0},{2,3},{3,2},{4,5},{5,4},{6,7},{7,6},{8,9},{9,8},{10,11... | collective-permute-start | bytes 122888 | tf_op jit(solution)/shard_map/ppermute | solution.py:213
  20.0 1.3 %collective-permute-start.9 = (bf16[80,256]{1,0:T(8,128)(2,1)S(1)}, bf16[80,256]{1,0:T(8,128)(2,1)S(1)}, u32[]{:S(2)}, u32[]{:S(2)}) collective-permute-start(bf16[80,256]{1,0:T(8,128)(2,1)S(1)} %collective-permute-done.1.refs_9_), channel_id=1, source_target_pairs={{0,1},{1,0},{2,3},{3,2},{4,5},{5,4},{6,7},{7,6},{8,9},{9,8},{10,11... | collective-permute-start | bytes 122888 | tf_op jit(solution)/shard_map/ppermute | solution.py:213
  20.5 1.2 %collective-permute-start.10 = (bf16[80,256]{1,0:T(8,128)(2,1)S(1)}, bf16[80,256]{1,0:T(8,128)(2,1)S(1)}, u32[]{:S(2)}, u32[]{:S(2)}) collective-permute-start(bf16[80,256]{1,0:T(8,128)(2,1)S(1)} %collective-permute-done.2.refs_11_), channel_id=1, source_target_pairs={{0,1},{1,0},{2,3},{3,2},{4,5},{5,4},{6,7},{7,6},{8,9},{9,8},{10,11... | collective-permute-start | bytes 122888 | tf_op jit(solution)/shard_map/ppermute | solution.py:213
where the time goes:
time: 25.1 us; the launch traced here: 24.9 us
  starting transfers between devices  14.9 us (59%)
  Pallas kernels  6.79 us (27%)
  waiting for transfers between devices  1.71 us (7%)
  local copies, waits for them, and re-layouts  0.79 us (3%)
  between operations  0.74 us (3%)
    ppermute x1, starting transfers between devices, on_device(): firsts.append(lax.ppermute(basis, ('sub', 'rhs', 'face'), pairs))  5.93 us
    ppermute x3, starting transfers between devices, on_device(): arrived.append(lax.ppermute(packs[shift], 'sub', ring))  4.62 us
    pallas_call x1, Pallas kernels, on_device(): pl.pallas_call(functools.partial(apply_kernel, groups), out_shape=jax.Sha...  3.21 us
    ppermute x1, starting transfers between devices, on_device(): second = lax.ppermute(first, 'rhs', cross)  3.2 us
    pallas_call x1, Pallas kernels, on_device(): pl.pallas_call(pack_kernel, out_shape=[jax.ShapeDtypeStruct((pack_rows, d...  1.98 us
    pallas_call x1, Pallas kernels, on_device(): pl.pallas_call(own_kernel, out_shape=[jax.ShapeDtypeStruct(block_shape, j...  1.61 us
    ppermute x3, waiting for transfers between devices, on_device(): weights += [array, lax.ppermute(array, 'face', swap)]  1.14 us
    unnamed x12, local copies, waits for them, and re-layouts  0.79 us
  transfers between devices with their start and end apart: 11, of which 5 were waited for; matrix products, arithmetic and copies ran while one was open for 0% of the time, Pallas kernels for 14%

commit v1 on v0

--- a/solution.py
+++ b/solution.py
@@ -15,14 +15,13 @@
 TILES = 4
 
 
-def pack_kernel(owner_ref, slot_ref, scale_ref, section_ref, *packs):
-    subdomains = len(packs)
-    rows, dof_count = packs[0].shape
+def pack_kernel(owner_ref, slot_ref, scale_ref, section_any, packs_ref, own_ref, section_ref, sem):
+    fetch = pltpu.make_async_copy(section_any, section_ref, sem)
+    fetch.start()
+    subdomains, rows, dof_count = packs_ref.shape
     rows -= ROW_TILE
     faces = owner_ref.shape[1]
-    sign = (1 - 2 * section_ref[...]).astype(jnp.float32)
-    shifts = lax.broadcasted_iota(jnp.int32, (subdomains, faces), 0)
-    named = lax.rem(lax.axis_index("sub") + shifts, subdomains) == owner_ref[...]
+    named = lax.broadcasted_iota(jnp.int32, (subdomains, faces), 0) == owner_ref[...]
     earlier = lax.broadcasted_iota(jnp.int32, (faces, faces), 0) < lax.broadcasted_iota(
         jnp.int32, (faces, faces), 1
     )
@@ -31,8 +30,10 @@
     )
     place = jnp.where(named, rank.astype(jnp.int32), -1)
     slots = slot_ref[...].astype(jnp.bfloat16)
-    for shift, pack_ref in enumerate(packs):
-        hit = place[shift : shift + 1, :] == lax.broadcasted_iota(jnp.int32, (rows, faces), 0)
+    fetch.wait()
+    sign = (1 - 2 * section_ref[0]).astype(jnp.float32)
+    for owner in range(subdomains):
+        hit = place[owner : owner + 1, :] == lax.broadcasted_iota(jnp.int32, (rows, faces), 0)
         hit = hit.astype(jnp.bfloat16)
         packed = jnp.dot(hit, scale_ref[...], preferred_element_type=jnp.float32) * sign
         listed = lax.dot_general(
@@ -40,8 +41,9 @@
         )
         meta = jnp.concatenate([listed, jnp.zeros((1, dof_count - rows), jnp.float32)], axis=1)
         meta = jnp.broadcast_to(meta, (ROW_TILE, dof_count))
-        pack_ref[:rows, :] = packed.astype(jnp.bfloat16)
-        pack_ref[rows:, :] = meta.astype(jnp.bfloat16)
+        packs_ref[owner, :rows, :] = packed.astype(jnp.bfloat16)
+        packs_ref[owner, rows:, :] = meta.astype(jnp.bfloat16)
+    own_ref[...] = packs_ref[lax.axis_index("sub")]
 
 
 def block_weights(packs, blocks_own):
@@ -95,7 +97,7 @@
 def apply_kernel(groups, *refs):
     pumped_ref, sum_ref, projection_ref = refs[:3]
     bases, refs = refs[3 : 3 + 4 * len(groups)], refs[3 + 4 * len(groups) :]
-    packs, (result_ref, weight_ref, basis_ref, scaled_ref, out_ref, sems) = refs[:-6], refs[-6:]
+    arrived_ref, swapped_ref, result_ref, weight_ref, basis_ref, scaled_ref, out_ref, sems = refs
     blocks_own, columns, dof_count = pumped_ref.shape
     others = weight_ref.shape[0]
     lane = 2 * lax.rem(lax.axis_index("rhs"), 2) + lax.axis_index("face")
@@ -115,7 +117,8 @@
         put(first_swapped, spare, a, c, b)
         put(second_swapped, c, b, spare, a)
     for other in range(others):
-        weight_ref[other] = block_weights(packs[2 * other : 2 * other + 2], blocks_own)
+        source = lax.rem(lax.axis_index("sub") + others - other, others + 1)
+        weight_ref[other] = block_weights((arrived_ref.at[source], swapped_ref.at[source]), blocks_own)
 
     tile_blocks = blocks_own // TILES
     copies = []
@@ -168,31 +171,26 @@
     for a, b, c in groups:
         pairs = []
         for s, r in cells:
-            for face, shift in ((0, b), (1, c)) if r % 2 else ((0, a),):
-                if shift < subdomains:
-                    pairs.append((flat(s, r, face), flat(s + shift, r, face)))
+            for face, shift in ((0, b), (1, c)) if r % 2 else ((0, a), (1, subdomains)):
+                pairs.append((flat(s, r, face), flat(s + shift, r, face)))
         firsts.append(lax.ppermute(basis, ("sub", "rhs", "face"), pairs))
 
-    packs = pl.pallas_call(
+    packs, own_pack = pl.pallas_call(
         pack_kernel,
-        out_shape=[jax.ShapeDtypeStruct((pack_rows, dof_count), jnp.bfloat16)] * subdomains,
-        in_specs=[VMEM] * 4,
-        out_specs=[VMEM] * subdomains,
+        out_shape=[
+            jax.ShapeDtypeStruct((subdomains, pack_rows, dof_count), jnp.bfloat16),
+            jax.ShapeDtypeStruct((pack_rows, dof_count), jnp.bfloat16),
+        ],
+        in_specs=[VMEM, VMEM, VMEM, HBM],
+        out_specs=[VMEM, VMEM],
+        scratch_shapes=[pltpu.SMEM((1,), jnp.int32), pltpu.SemaphoreType.DMA(())],
         cost_estimate=pl.CostEstimate(flops=4_000_000_000, bytes_accessed=8 * MIB, transcendentals=0),
         name="pack_weights",
-    )(
-        face_owner.reshape(1, faces_dev),
-        face_slot.reshape(1, faces_dev),
-        face_scale,
-        section.reshape(1, 1),
-    )
-    arrived = []
-    for shift in range(1, subdomains):
-        ring = [(i, (i + shift) % subdomains) for i in range(subdomains)]
-        arrived.append(lax.ppermute(packs[shift], "sub", ring))
-    own_swapped = lax.ppermute(packs[0], "face", swap)
-
-    firsts, own_pack = lax.optimization_barrier((firsts, packs[0]))
+    )(face_owner.reshape(1, faces_dev), face_slot.reshape(1, faces_dev), face_scale, section)
+    arrived = lax.all_to_all(packs, "sub", split_axis=0, concat_axis=0, tiled=True)
+    own_swapped = lax.ppermute(own_pack, "face", swap)
+
+    firsts, own_pack = lax.optimization_barrier((firsts, own_pack))
     pumped, own_sum = pl.pallas_call(
         own_kernel,
         out_shape=[
@@ -208,16 +206,14 @@
     )(mortar_in, pump_rate, well_cell, basis, own_pack, own_swapped)
 
     arrived, pumped = lax.optimization_barrier((arrived, pumped))
-    weights = []
-    for array in arrived:
-        weights += [array, lax.ppermute(array, "face", swap)]
+    swapped = lax.ppermute(arrived, "face", swap)
 
     bases = []
     for first in firsts:
         second = lax.ppermute(first, "rhs", cross)
         bases += [first, lax.ppermute(first, "face", swap), second, lax.ppermute(second, "face", swap)]
 
-    operands = [pumped, own_sum, projection, *bases, *weights]
+    operands = [pumped, own_sum, projection, *bases, arrived, swapped]
     return pl.pallas_call(
         functools.partial(apply_kernel, groups),
         out_shape=jax.ShapeDtypeStruct(block_shape, jnp.float32),

time: 25.1 us -> 26.1 us (1.040)
  starting transfers between devices: 14.9 us -> 12 us
  local copies, waits for them, and re-layouts: 0.79 us -> 3.28 us
  Pallas kernels: 6.79 us -> 8.1 us
    ppermute x7 -> x2, starting transfers between devices: 5.23 us -> 0.14 us  [the longest x1 0.07 us: on_device(): swapped = lax.ppermute(arrived, 'face', swap)]
    all_to_all x0 -> x1, starting transfers between devices: none -> 3.36 us  [on_device(): lax.all_to_all(packs, 'sub', split_axis=0, concat_axis=0, tiled=True)]
    unnamed x12, local copies, waits for them, and re-layouts: 0.79 us -> 3.28 us
    ppermute x7 -> x2, waiting for transfers between devices: 1.21 us -> 0.01 us  [the longest x1 0.01 us: on_device(): own_swapped = lax.ppermute(own_pack, 'face', swap)]
    ppermute x1, waiting for transfers between devices: 0.01 us -> 1.2 us  [on_device(): lax.ppermute(first, 'face', swap)]
    ppermute x1, starting transfers between devices: 3.2 us -> 2.04 us  [on_device(): second = lax.ppermute(first, 'rhs', cross)]
    pallas_call x1, Pallas kernels: 3.21 us -> 4.18 us  [on_device(): pl.pallas_call(functools.partial(apply_kernel, groups), out_shape=jax.Sha...]
    ppermute x1, starting transfers between devices: 0.01 us -> 0.5 us  [on_device(): lax.ppermute(first, 'face', swap)]
  transfers between devices with their start and end apart: 11 -> 7, of which waited for: 5 -> 2; matrix products, arithmetic and copies ran while one was open for 0% -> 0% of each run, Pallas kernels for 14% -> 15%
where the time goes in v1:
time: 26.1 us; the launch traced here: 25.7 us
  starting transfers between devices  12 us (46%)
  Pallas kernels  8.1 us (31%)
  local copies, waits for them, and re-layouts  3.28 us (13%)
  waiting for transfers between devices  1.49 us (6%)
  between operations  0.75 us (3%)
    ppermute x1, starting transfers between devices, on_device(): firsts.append(lax.ppermute(basis, ('sub', 'rhs', 'face'), pairs))  5.94 us
    pallas_call x1, Pallas kernels, on_device(): pl.pallas_call(functools.partial(apply_kernel, groups), out_shape=jax.Sha...  4.18 us
    all_to_all x1, starting transfers between devices, on_device(): lax.all_to_all(packs, 'sub', split_axis=0, concat_axis=0, tiled=True)  3.36 us
    unnamed x12, local copies, waits for them, and re-layouts  3.28 us
    pallas_call x1, Pallas kernels, on_device(): pl.pallas_call(pack_kernel, out_shape=[jax.ShapeDtypeStruct((subdomains,...  2.31 us
    ppermute x1, starting transfers between devices, on_device(): second = lax.ppermute(first, 'rhs', cross)  2.04 us
    pallas_call x1, Pallas kernels, on_device(): pl.pallas_call(own_kernel, out_shape=[jax.ShapeDtypeStruct(block_shape, j...  1.62 us
    ppermute x1, waiting for transfers between devices, on_device(): lax.ppermute(first, 'face', swap)  1.2 us
  transfers between devices with their start and end apart: 7, of which 2 were waited for; matrix products, arithmetic and copies ran while one was open for 0% of the time, Pallas kernels for 15%

profile of v1, /device:TPU:0, one launch (start us, length us, event | category | flops | bytes accessed | tf_op | source)
XLA Modules:
  0.0 25.7 jit_solution(7943171432358295015)
XLA Ops:
  0.0 5.9 %collective-permute-start = (bf16[1,256,256]{2,1,0:T(8,128)(2,1)}, bf16[1,256,256]{2,1,0:T(8,128)(2,1)}, u32[]{:S(2)}, u32[]{:S(2)}) collective-permute-start(bf16[1,256,256]{2,1,0:T(8,128)(2,1)} %basis_ref.1), channel_id=1, source_target_pairs={{0,8},{1,1},{2,6},{3,15},{4,12},{5,5},{6,10},{7,3},{8,0},{9,9},{10... | collective-permute-start | bytes 393224 | tf_op jit(solution)/shard_map/ppermute | solution.py:176
  6.6 0.0 copy-start.4
  6.6 0.0 copy-start.5
  6.6 2.3 %pack_weights.1 = (bf16[4,80,256]{2,1,0:T(8,128)(2,1)}, bf16[80,256]{1,0:T(8,128)(2,1)}) custom-call(s32[1,128]{1,0:T(1,128)} %bitcast.2, s32[1,128]{1,0:T(1,128)} %bitcast.3, bf16[128,256]{1,0:T(8,128)(2,1)} %scale_ref.1, s32[1]{0:T(128)S(6)} %copy.10.section_any), custom_call_target="tpu_custom_call" | custom-call | flops 4000000000 | bytes 8388608 | tf_op jit(solution)/shard_map/pack_weights/pallas_call | solution.py:178
  8.9 3.4 %all-to-all-start = ((bf16[4,80,256]{2,1,0:T(8,128)(2,1)}), bf16[4,80,256]{2,1,0:T(8,128)(2,1)S(1)}, u32[]{:S(2)}, u32[]{:S(2)}) async-start(bf16[4,80,256]{2,1,0:T(8,128)(2,1)} %get-tuple-element.13), calls=%async_computation | async-start | bytes 327680 | tf_op jit(solution)/shard_map/all_to_all | solution.py:190
  12.3 0.0 copy-start
  12.3 0.1 collective-permute-start.1
  12.4 0.0 collective-permute-done.refs_3_
  12.4 2.0 %collective-permute-start.3 = (bf16[1,256,256]{2,1,0:T(8,128)(2,1)}, bf16[1,256,256]{2,1,0:T(8,128)(2,1)}, u32[]{:S(2)}, u32[]{:S(2)}) collective-permute-start(bf16[1,256,256]{2,1,0:T(8,128)(2,1)} %collective-permute-done.refs_3_), channel_id=1, source_target_pairs={{0,2},{2,0},{1,3},{3,1},{4,6},{6,4},{5,7},{7,5},{8,10},{10,8},{9,1... | collective-permute-start | bytes 393224 | tf_op jit(solution)/shard_map/ppermute | solution.py:213
  14.4 0.0 collective-permute-done.1.swapped_ref
  14.4 0.0 copy-done.4
  14.4 0.0 copy-done.5
  14.4 0.0 copy-start.1
  14.5 1.6 %copy-done.1 = bf16[128,32,256]{2,1,0:T(8,128)(2,1)S(1)} copy-done((bf16[128,32,256]{2,1,0:T(8,128)(2,1)S(1)}, bf16[128,32,256]{2,1,0:T(8,128)(2,1)}, u32[]{:S(2)}) %copy-start.1) | copy-done | bytes 2097176
  16.0 0.0 copy-start.2
  16.0 0.9 %copy-done.2 = bf16[1,256,256]{2,1,0:T(8,128)(2,1)S(1)} copy-done((bf16[1,256,256]{2,1,0:T(8,128)(2,1)S(1)}, bf16[1,256,256]{2,1,0:T(8,128)(2,1)}, u32[]{:S(2)}) %copy-start.2) | copy-done | bytes 131096
  16.9 0.0 copy-start.3
  16.9 0.8 %copy-done.3 = bf16[80,256]{1,0:T(8,128)(2,1)S(1)} copy-done((bf16[80,256]{1,0:T(8,128)(2,1)S(1)}, bf16[80,256]{1,0:T(8,128)(2,1)}, u32[]{:S(2)}) %copy-start.3) | copy-done | bytes 40984
  17.7 1.6 %own_blocks.1 = (bf16[64,32,256]{2,1,0:T(8,128)(2,1)S(1)}, f32[64,32,256]{2,1,0:T(8,128)S(1)}) custom-call(bf16[128,32,256]{2,1,0:T(8,128)(2,1)S(1)} %copy-done.1, f32[32]{0:T(128)S(1)} %copy-done.4, s32[32]{0:T(128)S(1)} %copy-done.5, bf16[1,256,256]{2,1,0:T(8,128)(2,1)S(1)} %copy-done.2, bf16[80,256]{1,0:T(8,128)(2,1)S(1)} %copy-done.3, ...), custom_call_target="tpu_custom_call" | custom-call | flops 2000000000 | bytes 8388608 | tf_op jit(solution)/shard_map/own_blocks/pallas_call | solution.py:194
  19.3 0.0 all-to-all-done.refs_7_
  19.4 0.1 collective-permute-start.5
  19.4 0.5 %collective-permute-start.2 = (bf16[1,256,256]{2,1,0:T(8,128)(2,1)}, bf16[1,256,256]{2,1,0:T(8,128)(2,1)S(1)}, u32[]{:S(2)}, u32[]{:S(2)}) collective-permute-start(bf16[1,256,256]{2,1,0:T(8,128)(2,1)} %collective-permute-done.refs_3_), channel_id=1, source_target_pairs={{0,1},{1,0},{2,3},{3,2},{4,5},{5,4},{6,7},{7,6},{8,9},{9,8},{10,11... | collective-permute-start | bytes 393224 | tf_op jit(solution)/shard_map/ppermute | solution.py:214
  19.9 0.0 collective-permute-done.3.refs_5_
  19.9 0.1 collective-permute-start.4
  20.0 1.2 %collective-permute-done.2.refs_4_ = bf16[1,256,256]{2,1,0:T(8,128)(2,1)S(1)} collective-permute-done((bf16[1,256,256]{2,1,0:T(8,128)(2,1)}, bf16[1,256,256]{2,1,0:T(8,128)(2,1)S(1)}, u32[]{:S(2)}, u32[]{:S(2)}) %collective-permute-start.2) | collective-permute-done | bytes 131104 | tf_op jit(solution)/shard_map/ppermute | solution.py:214
  21.2 0.3 %collective-permute-done.4.refs_6_ = bf16[1,256,256]{2,1,0:T(8,128)(2,1)S(1)} collective-permute-done((bf16[1,256,256]{2,1,0:T(8,128)(2,1)}, bf16[1,256,256]{2,1,0:T(8,128)(2,1)S(1)}, u32[]{:S(2)}, u32[]{:S(2)}) %collective-permute-start.4) | collective-permute-done | bytes 131104 | tf_op jit(solution)/shard_map/ppermute | solution.py:214
  21.5 0.0 collective-permute-done.5.refs_8_
  21.5 0.0 copy-done
  21.5 4.2 %apply_blocks.1 = f32[64,32,256]{2,1,0:T(8,128)} custom-call(bf16[64,32,256]{2,1,0:T(8,128)(2,1)S(1)} %get-tuple-element.17.refs_0_, f32[64,32,256]{2,1,0:T(8,128)S(1)} %get-tuple-element.18.refs_1_, bf16[256,256]{1,0:T(8,128)(2,1)S(1)} %copy-done, bf16[1,256,256]{2,1,0:T(8,128)(2,1)} %collective-permute-done.refs_3_, ...), custom_call_target="tpu_custom_call" | custom-call | tf_op jit(solution)/shard_map/apply_blocks/pallas_call | solution.py:217
Async XLA Ops:
  0.0 12.4 %collective-permute-start = (bf16[1,256,256]{2,1,0:T(8,128)(2,1)}, bf16[1,256,256]{2,1,0:T(8,128)(2,1)}, u32[]{:S(2)}, u32[]{:S(2)}) collective-permute-start(bf16[1,256,256]{2,1,0:T(8,128)(2,1)} %basis_ref.1), channel_id=1, source_target_pairs={{0,8},{1,1},{2,6},{3,15},{4,12},{5,5},{6,10},{7,3},{8,0},{9,9},{10... | collective-permute-start | bytes 393224 | tf_op jit(solution)/shard_map/ppermute | solution.py:176
  6.6 7.8 %copy-start.4 = (f32[32]{0:T(128)S(1)}, f32[32]{0:T(128)}, u32[]{:S(2)}) copy-start(f32[32]{0:T(128)} %rate_ref.1) | copy-start | bytes 388
  6.6 7.8 %copy-start.5 = (s32[32]{0:T(128)S(1)}, s32[32]{0:T(128)}, u32[]{:S(2)}) copy-start(s32[32]{0:T(128)} %cell_ref.1) | copy-start | bytes 388
  8.9 10.4 %all-to-all-start = ((bf16[4,80,256]{2,1,0:T(8,128)(2,1)}), bf16[4,80,256]{2,1,0:T(8,128)(2,1)S(1)}, u32[]{:S(2)}, u32[]{:S(2)}) async-start(bf16[4,80,256]{2,1,0:T(8,128)(2,1)} %get-tuple-element.13), calls=%async_computation | async-start | bytes 327680 | tf_op jit(solution)/shard_map/all_to_all | solution.py:190
  12.3 9.2 %copy-start = (bf16[256,256]{1,0:T(8,128)(2,1)S(1)}, bf16[256,256]{1,0:T(8,128)(2,1)}, u32[]{:S(2)}) copy-start(bf16[256,256]{1,0:T(8,128)(2,1)} %refs_2_.1) | copy-start | bytes 393220
  12.3 2.1 %collective-permute-start.1 = (bf16[80,256]{1,0:T(8,128)(2,1)}, bf16[80,256]{1,0:T(8,128)(2,1)S(1)}, u32[]{:S(2)}, u32[]{:S(2)}) collective-permute-start(bf16[80,256]{1,0:T(8,128)(2,1)} %get-tuple-element.15.pack_ref), channel_id=1, source_target_pairs={{0,1},{1,0},{2,3},{3,2},{4,5},{5,4},{6,7},{7,6},{8,9},{9,8},{10,11... | collective-permute-start | bytes 122888 | tf_op jit(solution)/shard_map/ppermute | solution.py:191
  12.4 7.5 %collective-permute-start.3 = (bf16[1,256,256]{2,1,0:T(8,128)(2,1)}, bf16[1,256,256]{2,1,0:T(8,128)(2,1)}, u32[]{:S(2)}, u32[]{:S(2)}) collective-permute-start(bf16[1,256,256]{2,1,0:T(8,128)(2,1)} %collective-permute-done.refs_3_), channel_id=1, source_target_pairs={{0,2},{2,0},{1,3},{3,1},{4,6},{6,4},{5,7},{7,5},{8,10},{10,8},{9,1... | collective-permute-start | bytes 393224 | tf_op jit(solution)/shard_map/ppermute | solution.py:213
  14.4 1.6 %copy-start.1 = (bf16[128,32,256]{2,1,0:T(8,128)(2,1)S(1)}, bf16[128,32,256]{2,1,0:T(8,128)(2,1)}, u32[]{:S(2)}) copy-start(bf16[128,32,256]{2,1,0:T(8,128)(2,1)} %mortar_ref.1) | copy-start | bytes 6291460
  16.0 0.9 %copy-start.2 = (bf16[1,256,256]{2,1,0:T(8,128)(2,1)S(1)}, bf16[1,256,256]{2,1,0:T(8,128)(2,1)}, u32[]{:S(2)}) copy-start(bf16[1,256,256]{2,1,0:T(8,128)(2,1)} %basis_ref.1) | copy-start | bytes 393220
  16.9 0.8 %copy-start.3 = (bf16[80,256]{1,0:T(8,128)(2,1)S(1)}, bf16[80,256]{1,0:T(8,128)(2,1)}, u32[]{:S(2)}) copy-start(bf16[80,256]{1,0:T(8,128)(2,1)} %get-tuple-element.15.pack_ref) | copy-start | bytes 122884
  19.4 2.1 %collective-permute-start.5 = (bf16[4,80,256]{2,1,0:T(8,128)(2,1)S(1)}, bf16[4,80,256]{2,1,0:T(8,128)(2,1)S(1)}, u32[]{:S(2)}, u32[]{:S(2)}) collective-permute-start(bf16[4,80,256]{2,1,0:T(8,128)(2,1)S(1)} %all-to-all-done.refs_7_), channel_id=1, source_target_pairs={{0,1},{1,0},{2,3},{3,2},{4,5},{5,4},{6,7},{7,6},{8,9},{9,8},{10,11... | collective-permute-start | bytes 491528 | tf_op jit(solution)/shard_map/ppermute | solution.py:209
  19.4 1.8 %collective-permute-start.2 = (bf16[1,256,256]{2,1,0:T(8,128)(2,1)}, bf16[1,256,256]{2,1,0:T(8,128)(2,1)S(1)}, u32[]{:S(2)}, u32[]{:S(2)}) collective-permute-start(bf16[1,256,256]{2,1,0:T(8,128)(2,1)} %collective-permute-done.refs_3_), channel_id=1, source_target_pairs={{0,1},{1,0},{2,3},{3,2},{4,5},{5,4},{6,7},{7,6},{8,9},{9,8},{10,11... | collective-permute-start | bytes 393224 | tf_op jit(solution)/shard_map/ppermute | solution.py:214
  19.9 1.6 %collective-permute-start.4 = (bf16[1,256,256]{2,1,0:T(8,128)(2,1)}, bf16[1,256,256]{2,1,0:T(8,128)(2,1)S(1)}, u32[]{:S(2)}, u32[]{:S(2)}) collective-permute-start(bf16[1,256,256]{2,1,0:T(8,128)(2,1)} %collective-permute-done.3.refs_5_), channel_id=1, source_target_pairs={{0,1},{1,0},{2,3},{3,2},{4,5},{5,4},{6,7},{7,6},{8,9},{9,8},{10,11... | collective-permute-start | bytes 393224 | tf_op jit(solution)/shard_map/ppermute | solution.py:214

commit v2 on v0

v2 whole, which is shorter than its diff:
```python
import functools

import jax
import jax.numpy as jnp
from jax import lax
from jax.experimental import pallas as pl
from jax.experimental.pallas import tpu as pltpu
from jax.sharding import PartitionSpec as P

ROW_TILE = 16
VMEM = pl.BlockSpec(memory_space=pltpu.VMEM)
HBM = pl.BlockSpec(memory_space=pltpu.HBM)
SMEM = pl.BlockSpec(memory_space=pltpu.SMEM)
MIB = 1024 * 1024
TILES = 4


def pack_kernel(owner_ref, slot_ref, scale_ref, section_ref, basis_ref, *packs):
    subdomains = len(packs)
    rows, dof_count = packs[0].shape
    rows -= ROW_TILE
    faces = owner_ref.shape[1]
    half_rows = dof_count // 2
    half = pl.multiple_of(lax.axis_index("face") * half_rows, half_rows)
    sign = (1 - 2 * section_ref[...].reshape(1, 1)).astype(jnp.float32)
    partners = lax.broadcasted_iota(jnp.int32, (subdomains, faces), 0)
    named = (lax.axis_index("sub") ^ partners) == owner_ref[...]
    earlier = lax.broadcasted_iota(jnp.int32, (faces, faces), 0) < lax.broadcasted_iota(
        jnp.int32, (faces, faces), 1
    )
    rank = jnp.dot(
        named.astype(jnp.bfloat16), earlier.astype(jnp.bfloat16), preferred_element_type=jnp.float32
    )
    place = jnp.where(named, rank.astype(jnp.int32), -1)
    slots = slot_ref[...].astype(jnp.bfloat16)
    for partner, pack_ref in enumerate(packs):
        hit = place[partner : partner + 1, :] == lax.broadcasted_iota(jnp.int32, (rows, faces), 0)
        hit = hit.astype(jnp.bfloat16)
        packed = jnp.dot(hit, scale_ref[...], preferred_element_type=jnp.float32) * sign
        listed = lax.dot_general(
            slots, hit, (((1,), (1,)), ((), ())), preferred_element_type=jnp.float32
        )
        meta = jnp.concatenate([listed, jnp.zeros((1, dof_count - rows), jnp.float32)], axis=1)
        meta = jnp.broadcast_to(meta, (ROW_TILE, dof_count))
        pack_ref[:rows, :] = packed.astype(jnp.bfloat16)
        pack_ref[rows : rows + ROW_TILE, :] = meta.astype(jnp.bfloat16)
        if partner:
            pack_ref[rows + ROW_TILE :, :] = basis_ref[0, pl.ds(half, half_rows), :]


def block_weights(packs, rows, blocks_own):
    first = lax.axis_index("face") * blocks_own
    block_ids = first + lax.broadcasted_iota(jnp.int32, (blocks_own, rows), 0)
    total = None
    for pack in packs:
        slots = pack[rows : rows + ROW_TILE, :].astype(jnp.int32)[:1, :rows]
        hit = (slots == block_ids).astype(jnp.bfloat16)
        part = jnp.dot(hit, pack[:rows, :], preferred_element_type=jnp.float32)
        total = part if total is None else total + part
    return total


def own_kernel(mortar_ref, rate_ref, cell_ref, basis_ref, pack_ref, swapped_ref, pumped_ref, sum_ref, weight_ref, sem):
    blocks_own, columns, dof_count = pumped_ref.shape
    first_block = lax.axis_index("face") * blocks_own
    fetch = pltpu.make_async_copy(mortar_ref.at[pl.ds(first_block, blocks_own)], pumped_ref, sem)
    fetch.start()
    weight_ref[...] = block_weights((pack_ref, swapped_ref), pack_ref.shape[0] - ROW_TILE, blocks_own)
    fetch.wait()

    base = lax.axis_index("sub") * mortar_ref.shape[0] + first_block
    for column in range(columns):
        block = lax.div(cell_ref[column], dof_count) - base
        dof = lax.rem(cell_ref[column], dof_count)

        @pl.when((block >= 0) & (block < blocks_own))
        def _():
            slab = slice(column // ROW_TILE * ROW_TILE, (column // ROW_TILE + 1) * ROW_TILE)
            shape = (ROW_TILE, dof_count)
            at_well = (lax.broadcasted_iota(jnp.int32, shape, 0) == column % ROW_TILE) & (
                lax.broadcasted_iota(jnp.int32, shape, 1) == dof
            )
            well = jnp.where(at_well, rate_ref[column], 0.0)
            pumped_ref[block, slab, :] = (pumped_ref[block, slab, :].astype(jnp.float32) + well).astype(
                jnp.bfloat16
            )

    tile_blocks = blocks_own // TILES
    for tile in range(TILES):
        at = slice(tile * tile_blocks, (tile + 1) * tile_blocks)
        scaled = (pumped_ref[at].astype(jnp.float32) * weight_ref[at][:, None, :]).astype(jnp.bfloat16)
        flux = jnp.dot(
            scaled.reshape(tile_blocks * columns, dof_count), basis_ref[0], preferred_element_type=jnp.float32
        )
        sum_ref[at] = flux.reshape(tile_blocks, columns, dof_count)


def stage_kernel(count, last, pumped_ref, sum_ref, *refs):
    packs, refs = refs[: 2 * count], refs[2 * count :]
    if last:
        projection_ref, result_ref, weight_ref, basis_ref, scaled_ref, out_ref, sems = refs
    else:
        out_ref, weight_ref, basis_ref, scaled_ref = refs
    blocks_own, columns, dof_count = pumped_ref.shape
    half_rows = dof_count // 2
    rows = packs[0].shape[0] - ROW_TILE - half_rows
    for at in range(count):
        pair = packs[2 * at : 2 * at + 2]
        weight_ref[at] = block_weights(pair, rows, blocks_own)
        for which, pack in enumerate(pair):
            half = lax.axis_index("face") ^ which
            start = pl.multiple_of(at * dof_count + half * half_rows, half_rows)
            basis_ref[pl.ds(start, half_rows), :] = pack[rows + ROW_TILE :, :]

    tile_blocks = blocks_own // TILES
    copies = []
    for tile in range(TILES):
        at = slice(tile * tile_blocks, (tile + 1) * tile_blocks)
        values = pumped_ref[at].astype(jnp.float32)
        for other in range(count):
            scaled = (values * weight_ref[other, at][:, None, :]).astype(jnp.bfloat16)
            scaled_ref[tile % 2, :, other * dof_count : (other + 1) * dof_count] = scaled.reshape(
                tile_blocks * columns, dof_count
            )
        total = jnp.dot(scaled_ref[tile % 2], basis_ref[...], preferred_element_type=jnp.float32)
        total = total + sum_ref[at].reshape(tile_blocks * columns, dof_count)
        if last:
            total = jnp.dot(
                total.astype(jnp.bfloat16), projection_ref[...], preferred_element_type=jnp.float32
            )
        out_ref[at] = total.reshape(tile_blocks, columns, dof_count)
        if last:
            copies.append(pltpu.make_async_copy(out_ref.at[at], result_ref.at[at], sems.at[tile]))
            copies[-1].start()
    for copy in copies:
        copy.wait()


def on_device(
    mortar_in, pump_rate, well_cell, face_owner, face_slot, face_scale, section, basis, projection
):
    blocks_dev, cols_dev, dof_count = mortar_in.shape
    faces_dev = face_slot.shape[0]
    subdomains, halves = lax.axis_size("sub"), lax.axis_size("face")
    blocks_own = blocks_dev // halves
    capacity = max(2, 2 * faces_dev // subdomains)
    pack_rows = -(-capacity // ROW_TILE) * ROW_TILE + ROW_TILE
    block_shape = (blocks_own, cols_dev, dof_count)
    pack_shapes = [(pack_rows, dof_count)] + [(pack_rows + dof_count // halves, dof_count)] * (subdomains - 1)

    packs = pl.pallas_call(
        pack_kernel,
        out_shape=[jax.ShapeDtypeStruct(shape, jnp.bfloat16) for shape in pack_shapes],
        in_specs=[VMEM] * 5,
        out_specs=[VMEM] * subdomains,
        name="pack_weights",
    )(face_owner.reshape(1, faces_dev), face_slot.reshape(1, faces_dev), face_scale, section, basis)

    swap = [(i, i ^ 1) for i in range(halves)]
    partners = sorted(range(1, subdomains), key=lambda p: (p < subdomains // 2, p))
    arrived = {p: lax.ppermute(packs[p], "sub", [(i, i ^ p) for i in range(subdomains)]) for p in partners}
    own_swapped = lax.ppermute(packs[0], "face", swap)

    pumped, total = pl.pallas_call(
        own_kernel,
        out_shape=[
            jax.ShapeDtypeStruct(block_shape, jnp.bfloat16),
            jax.ShapeDtypeStruct(block_shape, jnp.float32),
        ],
        in_specs=[HBM, SMEM, SMEM, VMEM, VMEM, VMEM],
        out_specs=[VMEM, VMEM],
        scratch_shapes=[pltpu.VMEM((blocks_own, dof_count), jnp.float32), pltpu.SemaphoreType.DMA(())],
        compiler_params=pltpu.CompilerParams(vmem_limit_bytes=32 * MIB),
        cost_estimate=pl.CostEstimate(flops=2_000_000_000, bytes_accessed=8 * MIB, transcendentals=0),
        name="own_blocks",
    )(mortar_in, pump_rate, well_cell, basis, packs[0], own_swapped)

    for stage in (partners,):
        arrays, total = lax.optimization_barrier(([arrived[p] for p in stage], total))
        pairs = []
        for array in arrays:
            pairs += [array, lax.ppermute(array, "face", swap)]
        last = stage[-1] == partners[-1]
        count = len(stage)
        scratch = [
            pltpu.VMEM((count, blocks_own, dof_count), jnp.float32),
            pltpu.VMEM((count * dof_count, dof_count), jnp.bfloat16),
            pltpu.VMEM((2, blocks_own // TILES * cols_dev, count * dof_count), jnp.bfloat16),
        ]
        if last:
            scratch += [pltpu.VMEM(block_shape, jnp.float32), pltpu.SemaphoreType.DMA((TILES,))]
        operands = [pumped, total, *pairs] + ([projection] if last else [])
        total = pl.pallas_call(
            functools.partial(stage_kernel, count, last),
            out_shape=jax.ShapeDtypeStruct(block_shape, jnp.float32),
            in_specs=[VMEM] * len(operands),
            out_specs=HBM if last else VMEM,
            scratch_shapes=scratch,
            input_output_aliases={} if last else {1: 0},
            compiler_params=pltpu.CompilerParams(vmem_limit_bytes=40 * MIB),
            cost_estimate=pl.CostEstimate(flops=2_000_000_000, bytes_accessed=8 * MIB, transcendentals=0),
            name="last_stage" if last else "stage",
        )(*operands)
    return total


def solution(mesh):
    in_specs = (
        P(("groups", "sub"), "rhs", None),
        P(("groups", "rhs")),
        P(("groups", "rhs")),
        P(("groups", "sub", "face"), None),
        P(("groups", "sub", "face")),
        P(("groups", "sub", "face"), None),
        P(("groups", "sub")),
        P(("groups", "sub"), None, None),
        P(),
    )
    out_specs = P(("groups", "sub", "face"), "rhs", None)
    return jax.shard_map(
        on_device, mesh=mesh, in_specs=in_specs, out_specs=out_specs, check_vma=False
    )
```

time: 25.1 us -> 21.8 us (0.87)
  starting transfers between devices: 14.9 us -> 6.13 us
  local copies, waits for them, and re-layouts: 0.79 us -> 4.59 us
  waiting for transfers between devices: 1.71 us -> 3.3 us
    ppermute x10 -> x6, starting transfers between devices: 14.9 us -> 5.68 us  [the longest x3 5.17 us: on_device(): lax.ppermute(packs[p], 'sub', [(i, i ^ p) for i in range(subdomains)])]
    unnamed x12, local copies, waits for them, and re-layouts: 0.79 us -> 4.59 us
    ppermute x10 -> x6, waiting for transfers between devices: 1.71 us -> 3.3 us  [the longest x3 1.99 us: on_device(): lax.ppermute(packs[p], 'sub', [(i, i ^ p) for i in range(subdomains)])]
    ppermute x1, starting transfers between devices: 0.01 us -> 0.45 us  [on_device(): own_swapped = lax.ppermute(packs[0], 'face', swap)]
  transfers between devices with their start and end apart: 11 -> 7, of which waited for: 5 -> 5; matrix products, arithmetic and copies ran while one was open for 0% -> 0% of each run, Pallas kernels for 14% -> 7%
where the time goes in v2:
time: 21.8 us; the launch traced here: 21.5 us
  Pallas kernels  6.8 us (31%)
  starting transfers between devices  6.13 us (28%)
  local copies, waits for them, and re-layouts  4.59 us (21%)
  waiting for transfers between devices  3.3 us (15%)
  between operations  0.67 us (3%)
    ppermute x3, starting transfers between devices, on_device(): lax.ppermute(packs[p], 'sub', [(i, i ^ p) for i in range(subdomains)])  5.17 us
    unnamed x12, local copies, waits for them, and re-layouts  4.59 us
    pallas_call x1, Pallas kernels, on_device(): pl.pallas_call(functools.partial(stage_kernel, count, last), out_shape=ja...  3.22 us
    ppermute x3, waiting for transfers between devices, on_device(): lax.ppermute(packs[p], 'sub', [(i, i ^ p) for i in range(subdomains)])  1.99 us
    pallas_call x1, Pallas kernels, on_device(): pl.pallas_call(pack_kernel, out_shape=[jax.ShapeDtypeStruct(shape, jnp.bf...  1.98 us
    pallas_call x1, Pallas kernels, on_device(): pl.pallas_call(own_kernel, out_shape=[jax.ShapeDtypeStruct(block_shape, j...  1.6 us
    ppermute x3, waiting for transfers between devices, on_device(): pairs += [array, lax.ppermute(array, 'face', swap)]  1.31 us
    ppermute x3, starting transfers between devices, on_device(): pairs += [array, lax.ppermute(array, 'face', swap)]  0.51 us
  transfers between devices with their start and end apart: 7, of which 5 were waited for; matrix products, arithmetic and copies ran while one was open for 0% of the time, Pallas kernels for 7%

profile of v2, /device:TPU:0, one launch (start us, length us, event | category | flops | bytes accessed | tf_op | source)
XLA Modules:
  0.0 21.5 jit_solution(6168127552603785820)
XLA Ops:
  0.7 2.0 %pack_weights.1 = (bf16[80,256]{1,0:T(8,128)(2,1)}, bf16[208,256]{1,0:T(8,128)(2,1)}, bf16[208,256]{1,0:T(8,128)(2,1)}, bf16[208,256]{1,0:T(8,128)(2,1)}) custom-call(s32[1,128]{1,0:T(1,128)} %bitcast.2, s32[1,128]{1,0:T(1,128)} %bitcast.3, bf16[128,256]{1,0:T(8,128)(2,1)} %scale_ref.1, s32[1]{0:T(128)S(6)} %copy.10.section_ref, bf16[1,256,256]{2,1,0:T(8,128)(2,1)} %basis_ref.3), custom_call_target="tpu_custom_call" | custom-call | tf_op jit(solution)/shard_map/pack_weights/pallas_call | solution.py:151
  2.6 0.5 %collective-permute-start = (bf16[80,256]{1,0:T(8,128)(2,1)}, bf16[80,256]{1,0:T(8,128)(2,1)S(1)}, u32[]{:S(2)}, u32[]{:S(2)}) collective-permute-start(bf16[80,256]{1,0:T(8,128)(2,1)} %get-tuple-element.15.pack_ref), channel_id=1, source_target_pairs={{0,1},{1,0},{2,3},{3,2},{4,5},{5,4},{6,7},{7,6},{8,9},{9,8},{10,11... | collective-permute-start | bytes 122888 | tf_op jit(solution)/shard_map/ppermute | solution.py:162
  3.1 3.6 %collective-permute-start.1 = (bf16[208,256]{1,0:T(8,128)(2,1)}, bf16[208,256]{1,0:T(8,128)(2,1)S(1)}, u32[]{:S(2)}, u32[]{:S(2)}) collective-permute-start(bf16[208,256]{1,0:T(8,128)(2,1)} %get-tuple-element.17), channel_id=1, source_target_pairs={{0,8},{4,12},{8,0},{12,4},{1,9},{5,13},{9,1},{13,5},{2,10},{6,14},... | collective-permute-start | bytes 319496 | tf_op jit(solution)/shard_map/ppermute | solution.py:161
  6.7 1.3 %collective-permute-start.2 = (bf16[208,256]{1,0:T(8,128)(2,1)}, bf16[208,256]{1,0:T(8,128)(2,1)S(1)}, u32[]{:S(2)}, u32[]{:S(2)}) collective-permute-start(bf16[208,256]{1,0:T(8,128)(2,1)} %get-tuple-element.18), channel_id=1, source_target_pairs={{0,12},{4,8},{8,4},{12,0},{1,13},{5,9},{9,5},{13,1},{2,14},{6,10},... | collective-permute-start | bytes 319496 | tf_op jit(solution)/shard_map/ppermute | solution.py:161
  8.0 0.2 %collective-permute-start.3 = (bf16[208,256]{1,0:T(8,128)(2,1)}, bf16[208,256]{1,0:T(8,128)(2,1)S(1)}, u32[]{:S(2)}, u32[]{:S(2)}) collective-permute-start(bf16[208,256]{1,0:T(8,128)(2,1)} %get-tuple-element.19), channel_id=1, source_target_pairs={{0,4},{4,0},{8,12},{12,8},{1,5},{5,1},{9,13},{13,9},{2,6},{6,2},{1... | collective-permute-start | bytes 319496 | tf_op jit(solution)/shard_map/ppermute | solution.py:161
  8.3 0.0 collective-permute-done.swapped_ref
  8.3 0.0 copy-start
  8.3 0.9 %copy-done = bf16[1,256,256]{2,1,0:T(8,128)(2,1)S(1)} copy-done((bf16[1,256,256]{2,1,0:T(8,128)(2,1)S(1)}, bf16[1,256,256]{2,1,0:T(8,128)(2,1)}, u32[]{:S(2)}) %copy-start) | copy-done | bytes 131096
  9.2 0.0 copy-start.1
  9.2 1.6 %copy-done.1 = bf16[128,32,256]{2,1,0:T(8,128)(2,1)S(1)} copy-done((bf16[128,32,256]{2,1,0:T(8,128)(2,1)S(1)}, bf16[128,32,256]{2,1,0:T(8,128)(2,1)}, u32[]{:S(2)}) %copy-start.1) | copy-done | bytes 2097176
  10.8 0.0 copy-start.3
  10.8 0.8 %copy-done.3 = bf16[80,256]{1,0:T(8,128)(2,1)S(1)} copy-done((bf16[80,256]{1,0:T(8,128)(2,1)S(1)}, bf16[80,256]{1,0:T(8,128)(2,1)}, u32[]{:S(2)}) %copy-start.3) | copy-done | bytes 40984
  11.5 0.0 copy-start.4
  11.5 0.7 %copy-done.4 = f32[32]{0:T(128)S(1)} copy-done((f32[32]{0:T(128)S(1)}, f32[32]{0:T(128)}, u32[]{:S(2)}) %copy-start.4) | copy-done | bytes 152
  12.2 0.0 copy-start.5
  12.2 0.7 %copy-done.5 = s32[32]{0:T(128)S(1)} copy-done((s32[32]{0:T(128)S(1)}, s32[32]{0:T(128)}, u32[]{:S(2)}) %copy-start.5) | copy-done | bytes 152
  12.8 0.0 copy-start.2
  12.8 1.6 %own_blocks.1 = (bf16[64,32,256]{2,1,0:T(8,128)(2,1)S(1)}, f32[64,32,256]{2,1,0:T(8,128)S(1)}) custom-call(bf16[128,32,256]{2,1,0:T(8,128)(2,1)S(1)} %copy-done.1, f32[32]{0:T(128)S(1)} %copy-done.4, s32[32]{0:T(128)S(1)} %copy-done.5, bf16[1,256,256]{2,1,0:T(8,128)(2,1)S(1)} %copy-done, bf16[80,256]{1,0:T(8,128)(2,1)S(1)} %copy-done.3, ...), custom_call_target="tpu_custom_call" | custom-call | flops 2000000000 | bytes 8388608 | tf_op jit(solution)/shard_map/own_blocks/pallas_call | solution.py:164
  14.5 0.9 %collective-permute-done.1.refs_0_ = bf16[208,256]{1,0:T(8,128)(2,1)S(1)} collective-permute-done((bf16[208,256]{1,0:T(8,128)(2,1)}, bf16[208,256]{1,0:T(8,128)(2,1)S(1)}, u32[]{:S(2)}, u32[]{:S(2)}) %collective-permute-start.1) | collective-permute-done | bytes 106528 | tf_op jit(solution)/shard_map/ppermute | solution.py:161
  15.3 0.0 collective-permute-done.2.refs_2_
  15.3 1.1 %collective-permute-done.3.refs_4_ = bf16[208,256]{1,0:T(8,128)(2,1)S(1)} collective-permute-done((bf16[208,256]{1,0:T(8,128)(2,1)}, bf16[208,256]{1,0:T(8,128)(2,1)S(1)}, u32[]{:S(2)}, u32[]{:S(2)}) %collective-permute-start.3) | collective-permute-done | bytes 106528 | tf_op jit(solution)/shard_map/ppermute | solution.py:161
  16.5 0.0 collective-permute-start.4
  16.5 0.5 %collective-permute-start.5 = (bf16[208,256]{1,0:T(8,128)(2,1)S(1)}, bf16[208,256]{1,0:T(8,128)(2,1)S(1)}, u32[]{:S(2)}, u32[]{:S(2)}) collective-permute-start(bf16[208,256]{1,0:T(8,128)(2,1)S(1)} %collective-permute-done.2.refs_2_), channel_id=1, source_target_pairs={{0,1},{1,0},{2,3},{3,2},{4,5},{5,4},{6,7},{7,6},{8,9},{9,8},{10,11... | collective-permute-start | bytes 319496 | tf_op jit(solution)/shard_map/ppermute | solution.py:182
  17.0 0.0 collective-permute-start.6
  17.0 0.8 %collective-permute-done.4.refs_1_ = bf16[208,256]{1,0:T(8,128)(2,1)S(1)} collective-permute-done((bf16[208,256]{1,0:T(8,128)(2,1)S(1)}, bf16[208,256]{1,0:T(8,128)(2,1)S(1)}, u32[]{:S(2)}, u32[]{:S(2)}) %collective-permute-start.4) | collective-permute-done | bytes 106528 | tf_op jit(solution)/shard_map/ppermute | solution.py:182
  17.8 0.2 collective-permute-done.5.refs_3_
  17.9 0.4 %collective-permute-done.6.refs_5_ = bf16[208,256]{1,0:T(8,128)(2,1)S(1)} collective-permute-done((bf16[208,256]{1,0:T(8,128)(2,1)S(1)}, bf16[208,256]{1,0:T(8,128)(2,1)S(1)}, u32[]{:S(2)}, u32[]{:S(2)}) %collective-permute-start.6) | collective-permute-done | bytes 106528 | tf_op jit(solution)/shard_map/ppermute | solution.py:182
  18.3 0.0 copy-done.2
  18.3 3.2 %last_stage.1 = f32[64,32,256]{2,1,0:T(8,128)} custom-call(bf16[64,32,256]{2,1,0:T(8,128)(2,1)S(1)} %get-tuple-element.16.pumped_ref, f32[64,32,256]{2,1,0:T(8,128)S(1)} %get-tuple-element.21.sum_ref, bf16[208,256]{1,0:T(8,128)(2,1)S(1)} %collective-permute-done.1.refs_0_, bf16[208,256]{1,0:T(8,128)(2,1)S(1)} %collective-permute-done.4.refs_1_, ...), custom_call_target="tpu_custom_call" | custom-call | flops 2000000000 | bytes 8388608 | tf_op jit(solution)/shard_map/last_stage/pallas_call | solution.py:193
Async XLA Ops:
  2.6 5.6 %collective-permute-start = (bf16[80,256]{1,0:T(8,128)(2,1)}, bf16[80,256]{1,0:T(8,128)(2,1)S(1)}, u32[]{:S(2)}, u32[]{:S(2)}) collective-permute-start(bf16[80,256]{1,0:T(8,128)(2,1)} %get-tuple-element.15.pack_ref), channel_id=1, source_target_pairs={{0,1},{1,0},{2,3},{3,2},{4,5},{5,4},{6,7},{7,6},{8,9},{9,8},{10,11... | collective-permute-start | bytes 122888 | tf_op jit(solution)/shard_map/ppermute | solution.py:162
  3.1 12.2 %collective-permute-start.1 = (bf16[208,256]{1,0:T(8,128)(2,1)}, bf16[208,256]{1,0:T(8,128)(2,1)S(1)}, u32[]{:S(2)}, u32[]{:S(2)}) collective-permute-start(bf16[208,256]{1,0:T(8,128)(2,1)} %get-tuple-element.17), channel_id=1, source_target_pairs={{0,8},{4,12},{8,0},{12,4},{1,9},{5,13},{9,1},{13,5},{2,10},{6,14},... | collective-permute-start | bytes 319496 | tf_op jit(solution)/shard_map/ppermute | solution.py:161
  6.7 8.6 %collective-permute-start.2 = (bf16[208,256]{1,0:T(8,128)(2,1)}, bf16[208,256]{1,0:T(8,128)(2,1)S(1)}, u32[]{:S(2)}, u32[]{:S(2)}) collective-permute-start(bf16[208,256]{1,0:T(8,128)(2,1)} %get-tuple-element.18), channel_id=1, source_target_pairs={{0,12},{4,8},{8,4},{12,0},{1,13},{5,9},{9,5},{13,1},{2,14},{6,10},... | collective-permute-start | bytes 319496 | tf_op jit(solution)/shard_map/ppermute | solution.py:161
  8.0 8.4 %collective-permute-start.3 = (bf16[208,256]{1,0:T(8,128)(2,1)}, bf16[208,256]{1,0:T(8,128)(2,1)S(1)}, u32[]{:S(2)}, u32[]{:S(2)}) collective-permute-start(bf16[208,256]{1,0:T(8,128)(2,1)} %get-tuple-element.19), channel_id=1, source_target_pairs={{0,4},{4,0},{8,12},{12,8},{1,5},{5,1},{9,13},{13,9},{2,6},{6,2},{1... | collective-permute-start | bytes 319496 | tf_op jit(solution)/shard_map/ppermute | solution.py:161
  8.3 0.9 %copy-start = (bf16[1,256,256]{2,1,0:T(8,128)(2,1)S(1)}, bf16[1,256,256]{2,1,0:T(8,128)(2,1)}, u32[]{:S(2)}) copy-start(bf16[1,256,256]{2,1,0:T(8,128)(2,1)} %basis_ref.3) | copy-start | bytes 393220
  9.2 1.6 %copy-start.1 = (bf16[128,32,256]{2,1,0:T(8,128)(2,1)S(1)}, bf16[128,32,256]{2,1,0:T(8,128)(2,1)}, u32[]{:S(2)}) copy-start(bf16[128,32,256]{2,1,0:T(8,128)(2,1)} %mortar_ref.1) | copy-start | bytes 6291460
  10.8 0.8 %copy-start.3 = (bf16[80,256]{1,0:T(8,128)(2,1)S(1)}, bf16[80,256]{1,0:T(8,128)(2,1)}, u32[]{:S(2)}) copy-start(bf16[80,256]{1,0:T(8,128)(2,1)} %get-tuple-element.15.pack_ref) | copy-start | bytes 122884
  11.5 0.7 %copy-start.4 = (f32[32]{0:T(128)S(1)}, f32[32]{0:T(128)}, u32[]{:S(2)}) copy-start(f32[32]{0:T(128)} %rate_ref.1) | copy-start | bytes 388
  12.2 0.7 %copy-start.5 = (s32[32]{0:T(128)S(1)}, s32[32]{0:T(128)}, u32[]{:S(2)}) copy-start(s32[32]{0:T(128)} %cell_ref.1) | copy-start | bytes 388
  12.8 5.4 %copy-start.2 = (bf16[256,256]{1,0:T(8,128)(2,1)S(1)}, bf16[256,256]{1,0:T(8,128)(2,1)}, u32[]{:S(2)}) copy-start(bf16[256,256]{1,0:T(8,128)(2,1)} %refs_6_.1) | copy-start | bytes 393220
  16.5 1.3 %collective-permute-start.4 = (bf16[208,256]{1,0:T(8,128)(2,1)S(1)}, bf16[208,256]{1,0:T(8,128)(2,1)S(1)}, u32[]{:S(2)}, u32[]{:S(2)}) collective-permute-start(bf16[208,256]{1,0:T(8,128)(2,1)S(1)} %collective-permute-done.1.refs_0_), channel_id=1, source_target_pairs={{0,1},{1,0},{2,3},{3,2},{4,5},{5,4},{6,7},{7,6},{8,9},{9,8},{10,11... | collective-permute-start | bytes 319496 | tf_op jit(solution)/shard_map/ppermute | solution.py:182
  16.5 1.5 %collective-permute-start.5 = (bf16[208,256]{1,0:T(8,128)(2,1)S(1)}, bf16[208,256]{1,0:T(8,128)(2,1)S(1)}, u32[]{:S(2)}, u32[]{:S(2)}) collective-permute-start(bf16[208,256]{1,0:T(8,128)(2,1)S(1)} %collective-permute-done.2.refs_2_), channel_id=1, source_target_pairs={{0,1},{1,0},{2,3},{3,2},{4,5},{5,4},{6,7},{7,6},{8,9},{9,8},{10,11... | collective-permute-start | bytes 319496 | tf_op jit(solution)/shard_map/ppermute | solution.py:182
  17.0 1.3 %collective-permute-start.6 = (bf16[208,256]{1,0:T(8,128)(2,1)S(1)}, bf16[208,256]{1,0:T(8,128)(2,1)S(1)}, u32[]{:S(2)}, u32[]{:S(2)}) collective-permute-start(bf16[208,256]{1,0:T(8,128)(2,1)S(1)} %collective-permute-done.3.refs_4_), channel_id=1, source_target_pairs={{0,1},{1,0},{2,3},{3,2},{4,5},{5,4},{6,7},{7,6},{8,9},{9,8},{10,11... | collective-permute-start | bytes 319496 | tf_op jit(solution)/shard_map/ppermute | solution.py:182
